TPU v7x, 32 devices: a whole 2x2x4 slice. The times are simulated.
32 devices in a mesh: areal: 8 (over y, x, core), layer: 4 (over z).
Axes of the slice: x: 2, y: 2, z: 4, core: 2. Of those that a mesh axis runs over, the one named last changes fastest.
Arguments:
- pressure: float32 [32, 2048, 256], P('layer', 'areal'), may hold values from -6 to 6
- saturations: float32 [2, 32, 2048, 256], P(None, 'layer', 'areal'), may hold values from 0.05 to 0.4
- old_saturations: float32 [2, 32, 2048, 256], P(None, 'layer', 'areal'), may hold values from 0.05 to 0.4
- permeability: float32 [32, 2048, 256], P('layer', 'areal'), may hold values from 0.05 to 5
- pore_volume: float32 [32, 2048, 256], P('layer', 'areal'), may hold values from 0.5 to 2
- perf_cell: int32 [4, 8, 8, 256], P('layer', 'areal'), may hold values from 0 to 65535
- perf_layer: int32 [4, 8, 8, 256], P('layer', 'areal'), may hold values from 0 to 7
- perf_seg: int32 [4, 8, 8, 256], P('layer', 'areal'), may hold values from 0 to 383
- perf_index: float32 [4, 8, 8, 256], P('layer', 'areal'), may hold values from 0.5 to 4
- perf_blocks: int32 [4, 8, 8], P('layer', 'areal'), may hold values from 0 to 2, as said below
- seg_parent: int32 [1536, 8], P('areal'), may hold values from 0 to 6, as said below
- seg_cond: float32 [1536, 8], P('areal'), may hold values from 10 to 100
- seg_target: float32 [1536, 8], P('areal'), may hold values from -6 to 6
Outputs:
- cell_residual: float32 [3, 32, 2048, 256], P(None, 'layer', 'areal')
- well_pressure: float32 [1536, 8], P('areal', 'layer')
Inputs may be any that keep to these rules, and one draw needn't show every extreme that they name: `perf_blocks`: in every layer one owner index, drawn from the seed, has 2 live blocks from every areal index. Apart from it, each owner has 2 live blocks from its own areal index, 1 to 2 from the areal indices next to it (circularly), and 0 to 1 from the others. `seg_parent`: segment 0 has parent 0; every other segment's parent is a lower segment of the same well.
All inputs are finite; a program needn't handle non-finite values.
Results may differ from a plain program's by a relative error of at most 0.0003.
Values sent between devices are 32-bit elements; how exact they have to be, the bound alone decides.
A program may use at most 192 MiB of HBM per device.

v0:
```python
import functools

import jax
import jax.numpy as jnp
from jax import lax
from jax.experimental import pallas as pl
from jax.experimental.pallas import tpu as pltpu
from jax.sharding import PartitionSpec as P

BLOCK = 128
LANES = 128

MU_WATER = 0.5
MU_OIL = 2.0
MU_GAS = 0.2
GRAVITY = (0.35, 0.28, 0.07)
GEOMETRY = (0.4, 1.0, 1.0)
RELAX = 20.0

VMEM = pltpu.VMEM
SMEM = pltpu.SMEM
MESH = pl.DeviceIdType.MESH
VLIMIT = 56 * 1024 * 1024


def mobilities(water, gas_sat):
    oil_sat = 1.0 - water - gas_sat
    return (
        water * water * (1.0 / MU_WATER),
        oil_sat * oil_sat * (1.0 / MU_OIL),
        gas_sat * gas_sat * (1.0 / MU_GAS),
    )


def pieces(value):
    high = value.astype(jnp.bfloat16).astype(jnp.float32)
    rest = value - high
    mid = rest.astype(jnp.bfloat16).astype(jnp.float32)
    return high, mid, rest - mid


def panel_index(seg, slab, width):
    return (seg % slab) * width + seg // slab


def tall(value, rows):
    return jnp.concatenate(
        [value, jnp.zeros((rows - value.shape[0], value.shape[1]), value.dtype)], axis=0
    )


def column_part(row, part, halves):
    value = row[:, :LANES]
    for h in range(1, halves):
        value = jnp.where(part == h, row[:, h * LANES : (h + 1) * LANES], value)
    return value


def gather_kernel(
    slab, width, halves, flat_s, blocks_s, press, sats, flat, seg, index, blocks,
    sums, perf_press, perf_weight, rows,
):
    groups, slots = flat.shape
    for owner in range(groups):
        for block in range(slots // BLOCK):
            base = owner * slots + block * BLOCK

            @pl.when(blocks_s[owner] > block)
            def _(base=base, owner=owner, block=block):
                def step(i, carry):
                    for j in range(16):
                        at = i * 16 + j
                        number = flat_s[owner, block * BLOCK + at] // LANES
                        row = pl.ds(number // halves, 1)
                        part = number % halves
                        here = pl.ds(base + at, 1)
                        rows[0, here, :] = column_part(press[row, :], part, halves)
                        rows[1, here, :] = column_part(sats[0, row, :], part, halves)
                        rows[2, here, :] = column_part(sats[1, row, :], part, halves)
                    return carry

                lax.fori_loop(0, BLOCK // 16, step, 0)

    lanes_t = jnp.transpose(tall(flat[...] % LANES, LANES))
    lane = lax.broadcasted_iota(jnp.int32, (slots, LANES), 1)
    picked = jnp.zeros((slots, LANES), jnp.float32)
    for owner in range(groups):
        mask = lane == lanes_t[:, owner : owner + 1]
        for field in range(3):
            row = rows[field, owner * slots : (owner + 1) * slots, :]
            value = jnp.sum(jnp.where(mask, row, 0.0), axis=1, keepdims=True)
            picked = jnp.where(lane == field * groups + owner, value, picked)
    picked = jnp.transpose(picked)
    live = lax.broadcasted_iota(jnp.int32, (groups, slots), 1) < blocks[...] * BLOCK
    pressure = jnp.where(live, picked[0:groups], 0.0)
    water = picked[groups : 2 * groups]
    gas_sat = picked[2 * groups : 3 * groups]
    weight = jnp.where(live, index[...], 0.0)
    lam = mobilities(water, gas_sat)
    mobile = jnp.where(live, weight * lam[0] + weight * lam[1] + weight * lam[2], 0.0)
    perf_press[...] = pressure
    perf_weight[...] = weight
    parts = pieces(mobile) + pieces(mobile * pressure)
    target = panel_index(seg[...], slab, width)
    bins = lax.broadcasted_iota(jnp.int32, (slab * width, slots), 0)
    zero = jnp.zeros((2, slots), jnp.float32)
    chunks = slab * width // LANES
    for owner in range(groups):
        left = jnp.concatenate([part[owner : owner + 1] for part in parts] + [zero], axis=0)
        hot = jnp.where(bins == target[owner : owner + 1], 1.0, 0.0).astype(jnp.bfloat16)
        total = lax.dot_general(
            left.astype(jnp.bfloat16), hot, (((1,), (1,)), ((), ())),
            preferred_element_type=jnp.float32,
        )
        for kind in range(2):
            line = total[3 * kind : 3 * kind + 1] + total[3 * kind + 1 : 3 * kind + 2]
            line = line + total[3 * kind + 2 : 3 * kind + 3]
            for c in range(chunks):
                sums[owner, kind * chunks + c : kind * chunks + c + 1, :] = line[
                    :, c * LANES : (c + 1) * LANES
                ]


def wells_kernel(
    groups, layers, slab, width, sums, params, first, last,
    table, own_slab, before, after,
    got, panel, solved, send_a, recv_a, send_l, recv_l, send_p, recv_p, send_x, recv_x,
):
    area = lax.axis_index("areal")
    layer = lax.axis_index("layer")
    nseg = layers * slab
    half = width // LANES

    def areal_peer(d):
        return {"areal": lax.rem(area + d, groups)}

    def layer_peer(d):
        return {"layer": lax.rem(layer + d, layers)}

    barrier = pltpu.get_barrier_semaphore()
    for d in range(1, groups):
        pl.semaphore_signal(barrier, inc=1, device_id=areal_peer(d), device_id_type=MESH)
    for d in range(1, layers):
        pl.semaphore_signal(barrier, inc=1, device_id=layer_peer(d), device_id_type=MESH)
    pl.semaphore_wait(barrier, groups + layers - 2)

    to_owner = []
    for d in range(1, groups):
        copy = pltpu.make_async_remote_copy(
            sums.at[lax.rem(area + d, groups)], got.at[d], send_a.at[d], recv_a.at[d],
            device_id=areal_peer(d), device_id_type=MESH,
        )
        copy.start()
        to_owner.append(copy)
    halo = [
        pltpu.make_async_remote_copy(
            last, before, send_x.at[0], recv_x.at[0],
            device_id=areal_peer(1), device_id_type=MESH,
        ),
        pltpu.make_async_remote_copy(
            first, after, send_x.at[1], recv_x.at[1],
            device_id=areal_peer(groups - 1), device_id_type=MESH,
        ),
    ]
    for copy in halo:
        copy.start()

    total = sums[area]
    for d in range(1, groups):
        to_owner[d - 1].wait_recv()
        total = total + got[d]
    panel[layer] = total
    to_layers = []
    for d in range(1, layers):
        copy = pltpu.make_async_remote_copy(
            panel.at[layer], panel.at[layer], send_l.at[d], recv_l.at[d],
            device_id=layer_peer(d), device_id_type=MESH,
        )
        copy.start()
        to_layers.append(copy)
    for copy in to_layers:
        copy.wait_recv()

    def lines(kind):
        out = []
        for j in range(layers):
            tile = panel[j]
            for s in range(slab):
                at = (kind * slab + s) * half
                out.append(
                    jnp.concatenate([tile[at + h : at + h + 1] for h in range(half)], axis=1)
                )
        return jnp.concatenate(out, axis=0)

    excess = lines(0) + RELAX
    right = lines(1) + RELAX * params[2]
    parent = params[0]
    cond = params[1]
    place = lax.broadcasted_iota(jnp.int32, (nseg, width), 0).astype(jnp.float32)
    inverse = [None] * nseg
    hits = [None] * nseg
    for s in range(nseg - 1, 0, -1):
        c = cond[s : s + 1]
        e = excess[s : s + 1]
        inverse[s] = 1.0 / (e + c)
        ratio = c * inverse[s]
        hits[s] = place == parent[s : s + 1]
        excess = excess + jnp.where(hits[s], ratio * e, 0.0)
        right = right + jnp.where(hits[s], ratio * right[s : s + 1], 0.0)
    answer = jnp.where(place == 0.0, right[0:1] / excess[0:1], 0.0)
    for s in range(1, nseg):
        above = jnp.sum(jnp.where(hits[s], answer, 0.0), axis=0, keepdims=True)
        value = (right[s : s + 1] + cond[s : s + 1] * above) * inverse[s]
        answer = jnp.where(place == float(s), value, answer)
    for j in range(layers):
        solved[j] = answer[j * slab : (j + 1) * slab]
    mine = solved[layer]
    own_slab[...] = mine
    table[area] = mine
    back = []
    for d in range(1, groups):
        copy = pltpu.make_async_remote_copy(
            table.at[area], table.at[area], send_p.at[d], recv_p.at[d],
            device_id=areal_peer(d), device_id_type=MESH,
        )
        copy.start()
        back.append(copy)
    for copy in back:
        copy.wait_recv()
    for copy in halo:
        copy.wait()
    for copy in to_owner + to_layers + back:
        copy.wait_send()


def face_terms(geometry, left, right, kinds):
    trans = (geometry * 2.0) * (left[1] * right[1]) / (left[1] + right[1])
    drop = left[0] - right[0]
    if kinds is None:
        up = drop > 0
        flow = trans * drop
        return [flow * jnp.where(up, left[2][a], right[2][a]) for a in range(3)]
    out = []
    for a in range(3):
        potential = drop + kinds[a]
        out.append(trans * potential * jnp.where(potential > 0, left[2][a], right[2][a]))
    return out


def residual_kernel(
    slab, width, chunk, groups_count,
    flat_s, blocks_s, flat, seg, perf_press, perf_weight, table, press, sats, perm, before, after,
    old, pore, out, source, adds, lower,
):
    level = pl.program_id(0)
    depth, nx, ny = press.shape
    groups, slots = flat.shape

    @pl.when(level == 0)
    def _():
        source[...] = jnp.zeros_like(source)
        lower[...] = jnp.zeros_like(lower)
        target = panel_index(seg[...], slab, width)
        bins = lax.broadcasted_iota(jnp.int32, (slab * width, slots), 0)
        found = []
        for owner in range(groups):
            tab = table[owner]
            line = jnp.concatenate([tab[s : s + 1] for s in range(slab)], axis=1)
            left = jnp.concatenate(
                list(pieces(line)) + [jnp.zeros((5, slab * width), jnp.float32)], axis=0
            )
            hot = jnp.where(bins == target[owner : owner + 1], 1.0, 0.0).astype(jnp.bfloat16)
            value = jnp.dot(left.astype(jnp.bfloat16), hot, preferred_element_type=jnp.float32)
            found.append(value[0:1] + value[1:2] + value[2:3])
        rate = perf_weight[...] * (perf_press[...] - jnp.concatenate(found, axis=0))
        rate_t = jnp.transpose(tall(rate, LANES))
        lanes_t = jnp.transpose(tall(flat[...] % ny, LANES))
        lane = lax.broadcasted_iota(jnp.int32, (slots, ny), 1)
        for owner in range(groups):
            adds[owner * slots : (owner + 1) * slots, :] = jnp.where(
                lane == lanes_t[:, owner : owner + 1], rate_t[:, owner : owner + 1], 0.0
            )
        for owner in range(groups):
            for block in range(slots // BLOCK):
                base = owner * slots + block * BLOCK

                @pl.when(blocks_s[owner] > block)
                def _(base=base, owner=owner, block=block):
                    def step(i, carry):
                        for j in range(16):
                            at = i * 16 + j
                            number = flat_s[owner, block * BLOCK + at] // ny
                            row = pl.ds(number, 1)
                            source[row, :] = source[row, :] + adds[pl.ds(base + at, 1), :]
                        return carry

                    lax.fori_loop(0, BLOCK // 16, step, 0)

    area = lax.axis_index("areal")
    above = jnp.minimum(level + 1, depth - 1)
    inner = jnp.where(level + 1 < depth, GEOMETRY[0], 0.0)
    row_from = pl.multiple_of(level * nx, nx)

    def edge(halo, real):
        values = [halo[f, pl.ds(level, 1), :] for f in range(4)]
        return (values[0], jnp.where(real, values[3], 0.0), mobilities(values[1], values[2]))

    def line(x):
        return (
            press[level, x : x + 1, :],
            perm[level, x : x + 1, :],
            mobilities(sats[0, level, x : x + 1, :], sats[1, level, x : x + 1, :]),
        )

    carry = face_terms(GEOMETRY[1], edge(before, area > 0), line(0), None)
    column = lax.broadcasted_iota(jnp.int32, (chunk, ny), 1)
    for x in range(0, nx, chunk):
        span = slice(x, x + chunk)
        p = press[level, span, :]
        water = sats[0, level, span, :]
        gas_sat = sats[1, level, span, :]
        k = perm[level, span, :]
        lam = mobilities(water, gas_sat)
        here = (p, k, lam)
        beyond = line(x + chunk) if x + chunk < nx else edge(after, area < groups_count - 1)

        def shifted(value, row):
            return jnp.concatenate([value[1:], row], axis=0)

        there = (
            shifted(p, beyond[0]),
            shifted(k, beyond[1]),
            tuple(shifted(lam[a], beyond[2][a]) for a in range(3)),
        )
        flux = face_terms(GEOMETRY[1], here, there, None)
        total = []
        for a in range(3):
            total.append(flux[a] - jnp.concatenate([carry[a], flux[a][:-1]], axis=0))
        carry = [flux[a][chunk - 1 :] for a in range(3)]
        there = (
            pltpu.roll(p, ny - 1, 1),
            jnp.where(column < ny - 1, pltpu.roll(k, ny - 1, 1), 0.0),
            tuple(pltpu.roll(lam[a], ny - 1, 1) for a in range(3)),
        )
        flux = face_terms(GEOMETRY[2], here, there, None)
        for a in range(3):
            total[a] = total[a] + (flux[a] - pltpu.roll(flux[a], 1, 1))
        there = (
            press[above, span, :],
            perm[above, span, :],
            mobilities(sats[0, above, span, :], sats[1, above, span, :]),
        )
        flux = face_terms(inner, here, there, GRAVITY)
        well = source[pl.ds(row_from + x, chunk), :]
        volume = pore[0, span, :]
        old_water = old[0, 0, span, :]
        old_gas = old[1, 0, span, :]
        change = (
            water - old_water,
            (1.0 - water - gas_sat) - (1.0 - old_water - old_gas),
            gas_sat - old_gas,
        )
        for a in range(3):
            net = total[a] + (flux[a] - lower[a, span, :])
            lower[a, span, :] = flux[a]
            out[a, 0, span, :] = volume * change[a] + net + lam[a] * well


def ends_kernel(depth, given, press, sats, perm, below, over, out):
    rows = press.shape[1]
    chunk = 16
    end = pl.program_id(0)
    for x in range(0, rows, chunk):
        span = slice(x, x + chunk)
        here = (press[0, span, :], perm[0, span, :], mobilities(sats[0, 0, span, :], sats[1, 0, span, :]))

        def other(ref):
            return (ref[0, span, :], ref[3, span, :], mobilities(ref[1, span, :], ref[2, span, :]))

        @pl.when(end == 0)
        def _():
            flux = face_terms(GEOMETRY[0], other(below), here, GRAVITY)
            for a in range(3):
                out[a, 0, span, :] = given[a, 0, span, :] - flux[a]

        @pl.when(end == 1)
        def _():
            flux = face_terms(GEOMETRY[0], here, other(over), GRAVITY)
            for a in range(3):
                out[a, 0, span, :] = given[a, 0, span, :] + flux[a]


def on_device(
    pressure,
    saturations,
    old_saturations,
    permeability,
    pore_volume,
    perf_cell,
    perf_layer,
    perf_seg,
    perf_index,
    perf_blocks,
    seg_parent,
    seg_cond,
    seg_target,
):
    f32 = jnp.float32
    depth, nx, ny = pressure.shape
    groups, slots = perf_cell.shape[2:]
    layers = lax.axis_size("layer")
    wells, nseg = seg_parent.shape
    slab = nseg // layers
    width = -(-wells // LANES) * LANES
    halves = ny // LANES
    shape = jax.ShapeDtypeStruct
    vm = pl.BlockSpec(memory_space=VMEM)
    sm = pl.BlockSpec(memory_space=SMEM)

    up = [(i, i + 1) for i in range(layers - 1)]
    down = [(j, i) for i, j in up]
    top = jnp.concatenate([pressure[-1:], saturations[:, -1], permeability[-1:]], axis=0)
    bottom = jnp.concatenate([pressure[:1], saturations[:, 0], permeability[:1]], axis=0)
    below = lax.ppermute(top, "layer", up)
    over = lax.ppermute(bottom, "layer", down)

    flat = perf_layer[0, 0] * (nx * ny) + perf_cell[0, 0]
    seg = perf_seg[0, 0]
    count = perf_blocks[0, 0]
    tiles = 2 * slab * width // LANES
    sums, perf_press, perf_weight = pl.pallas_call(
        functools.partial(gather_kernel, slab, width, halves),
        out_shape=(
            shape((groups, tiles, LANES), f32),
            shape((groups, slots), f32),
            shape((groups, slots), f32),
        ),
        in_specs=[sm, sm] + [vm] * 6,
        out_specs=(vm, vm, vm),
        scratch_shapes=[VMEM((3, groups * slots, LANES), f32)],
        compiler_params=pltpu.CompilerParams(vmem_limit_bytes=VLIMIT),
        cost_estimate=pl.CostEstimate(flops=10**7, bytes_accessed=3 * 10**7, transcendentals=0),
        name="gather_perforations",
    )(
        flat, count, pressure.reshape(depth * nx, ny), saturations.reshape(2, depth * nx, ny),
        flat, seg, perf_index[0, 0], count[:, None],
    )

    params = jnp.stack([seg_parent.astype(f32), seg_cond, seg_target]).transpose(0, 2, 1)
    params = jnp.pad(params, ((0, 0), (0, 0), (0, width - wells)), constant_values=1.0)
    first = jnp.concatenate(
        [pressure[None, :, 0], saturations[:, :, 0], permeability[None, :, 0]], axis=0
    )
    last = jnp.concatenate(
        [pressure[None, :, -1], saturations[:, :, -1], permeability[None, :, -1]], axis=0
    )
    dma = pltpu.SemaphoreType.DMA
    table, own_slab, before, after = pl.pallas_call(
        functools.partial(wells_kernel, groups, layers, slab, width),
        out_shape=(
            shape((groups, slab, width), f32),
            shape((slab, width), f32),
            shape(first.shape, f32),
            shape(first.shape, f32),
        ),
        in_specs=[vm] * 4,
        out_specs=(vm,) * 4,
        scratch_shapes=[
            VMEM((groups, tiles, LANES), f32),
            VMEM((layers, tiles, LANES), f32),
            VMEM((layers, slab, width), f32),
            dma((groups,)), dma((groups,)),
            dma((layers,)), dma((layers,)),
            dma((groups,)), dma((groups,)),
            dma((2,)), dma((2,)),
        ],
        compiler_params=pltpu.CompilerParams(collective_id=0, has_side_effects=True),
        cost_estimate=pl.CostEstimate(flops=10**6, bytes_accessed=10**7, transcendentals=0),
        name="solve_wells",
    )(sums, params, first, last)

    plane = lambda n: pl.BlockSpec((n, 1, nx, ny), lambda i: (0, i, 0, 0))
    residual = pl.pallas_call(
        functools.partial(residual_kernel, slab, width, 16, groups),
        grid=(depth,),
        out_shape=shape((3, depth, nx, ny), f32),
        in_specs=[sm, sm] + [vm] * 10 + [plane(2), pl.BlockSpec((1, nx, ny), lambda i: (i, 0, 0))],
        out_specs=plane(3),
        scratch_shapes=[
            VMEM((depth * nx, ny), f32),
            VMEM((groups * slots, ny), f32),
            VMEM((3, nx, ny), f32),
        ],
        compiler_params=pltpu.CompilerParams(
            vmem_limit_bytes=VLIMIT, dimension_semantics=("arbitrary",)
        ),
        cost_estimate=pl.CostEstimate(flops=10**8, bytes_accessed=6 * 10**7, transcendentals=0),
        name="cell_residual",
    )(
        flat, count, flat, seg, perf_press, perf_weight, table,
        pressure, saturations, permeability, before, after, old_saturations, pore_volume,
    )

    part = 64 if nx % 64 == 0 else nx
    ends = lambda n: pl.BlockSpec((n, 1, part, ny), lambda e, j: (0, e * (depth - 1), j, 0))
    flat_end = pl.BlockSpec((1, part, ny), lambda e, j: (e * (depth - 1), j, 0))
    halo = pl.BlockSpec((4, part, ny), lambda e, j: (0, j, 0))
    residual = pl.pallas_call(
        functools.partial(ends_kernel, depth),
        grid=(2, nx // part),
        out_shape=shape(residual.shape, f32),
        in_specs=[ends(3), flat_end, ends(2), flat_end, halo, halo],
        out_specs=ends(3),
        input_output_aliases={0: 0},
        compiler_params=pltpu.CompilerParams(dimension_semantics=("arbitrary", "arbitrary")),
        cost_estimate=pl.CostEstimate(flops=10**7, bytes_accessed=8 * 10**6, transcendentals=0),
        name="outer_layers",
    )(residual, pressure, saturations, permeability, below, over)
    return residual, own_slab[:, :wells].T


def solution(mesh):
    return jax.shard_map(
        on_device,
        mesh=mesh,
        in_specs=(
            P("layer", "areal", None),
            P(None, "layer", "areal", None),
            P(None, "layer", "areal", None),
            P("layer", "areal", None),
            P("layer", "areal", None),
            P("layer", "areal", None, None),
            P("layer", "areal", None, None),
            P("layer", "areal", None, None),
            P("layer", "areal", None, None),
            P("layer", "areal", None),
            P("areal", None),
            P("areal", None),
            P("areal", None),
        ),
        out_specs=(P(None, "layer", "areal", None), P("areal", "layer")),
        check_vma=False,
    )
```

profile of v0, /device:TPU:1, one launch (start us, length us, event | category | flops | bytes accessed | tf_op | source)
XLA Modules:
  0.0 99.5 jit_solution(10370259796853026896)
XLA Ops:
  0.6 1.3 %slice_bitcast_fusion = (f32[2,256,256]{2,1,0:T(8,128)S(1)}, f32[2,256,256]{2,1,0:T(8,128)S(1)}) fusion(f32[2,8,256,256]{3,2,1,0:T(8,128)} %sats.3), kind=kLoop, calls=%fused_computation.2 | loop fusion | bytes 2097152 | tf_op jit(solution)/shard_map/squeeze | solution.py:423
  1.9 1.3 %fusion.1 = (f32[1,256,256]{2,1,0:T(8,128)S(1)}, f32[1,256,256]{2,1,0:T(8,128)S(1)}, f32[1,256,256]{2,1,0:T(8,128)S(1)}, f32[1,256,256]{2,1,0:T(8,128)S(1)}) fusion(f32[8,256,256]{2,1,0:T(8,128)} %press.3, f32[8,256,256]{2,1,0:T(8,128)} %perm.3), kind=kLoop, calls=%fused_computation.17 | loop fusion | bytes 2097152 | tf_op jit(solution)/shard_map/slice | solution.py:423
  3.2 0.0 copy-start.2
  3.2 0.0 copy-start.3
  3.3 0.0 copy-start.6
  3.3 0.1 pad_maximum_fusion
  3.4 4.1 %collective-permute-start = (f32[4,256,256]{2,1,0:T(8,128)S(1)}, f32[4,256,256]{2,1,0:T(8,128)S(1)}, u32[]{:S(2)}, u32[]{:S(2)}) collective-permute-start(f32[4,256,256]{2,1,0:T(8,128)S(1)} %pad_maximum_fusion), channel_id=1, source_target_pairs={{0,1},{1,2},{2,3},{4,5},{5,6},{6,7},{8,9},{9,10},{10,11},{12,13},{... | collective-permute-start | bytes 3145736 | tf_op jit(solution)/shard_map/ppermute | solution.py:424
  7.5 1.1 %pad_maximum_fusion.1 = f32[4,256,256]{2,1,0:T(8,128)} fusion(f32[1,256,256]{2,1,0:T(8,128)S(1)} %get-tuple-element.35, f32[2,256,256]{2,1,0:T(8,128)S(1)} %get-tuple-element.16, f32[1,256,256]{2,1,0:T(8,128)S(1)} %get-tuple-element.20), kind=kLoop, calls=%fused_computation.1 | loop fusion | flops 524288 | bytes 2097152 | tf_op jit(solution)/shard_map/concatenate | solution.py:423
  8.5 1.3 %collective-permute-start.1 = (f32[4,256,256]{2,1,0:T(8,128)}, f32[4,256,256]{2,1,0:T(8,128)S(1)}, u32[]{:S(2)}, u32[]{:S(2)}) collective-permute-start(f32[4,256,256]{2,1,0:T(8,128)} %pad_maximum_fusion.1), channel_id=1, source_target_pairs={{1,0},{2,1},{3,2},{5,4},{6,5},{7,6},{9,8},{10,9},{11,10},{13,12},{... | collective-permute-start | bytes 3145736 | tf_op jit(solution)/shard_map/ppermute | solution.py:425
  9.8 0.9 fusion.4
  10.7 0.9 fusion.3
  11.6 0.7 copy.16.blocks
  12.3 0.6 add_bitcast_fusion.flat_s.flat
  12.9 0.6 pad.4.params
  13.6 24.2 %gather_perforations.1 = (f32[8,8,128]{2,1,0:T(8,128)}, f32[8,256]{1,0:T(8,128)}, f32[8,256]{1,0:T(8,128)}) custom-call(s32[8,256]{1,0:T(8,128)} %add_bitcast_fusion.flat_s.flat, s32[8]{0:T(128)} %bitcast.43, f32[2048,256]{1,0:T(8,128)} %bitcast.37, f32[2,2048,256]{2,1,0:T(8,128)} %bitcast.36, s32[8,256]{1,0:T(8,128)} %add_bitcast_fusion.flat_s.flat, ...), custom_call_target="tpu_custom_call" | custom-call | flops 10000000 | bytes 30000000 | tf_op jit(solution)/shard_map/gather_perforations/pallas_call | solution.py:431
  37.7 1.0 fusion
  38.7 0.6 pad_maximum_fusion.3.last
  39.4 0.6 pad_maximum_fusion.2.first
  40.0 19.3 %solve_wells.1 = (f32[8,2,256]{2,1,0:T(2,128)}, f32[2,256]{1,0:T(2,128)}, f32[4,8,256]{2,1,0:T(8,128)}, f32[4,8,256]{2,1,0:T(8,128)}) custom-call(f32[8,8,128]{2,1,0:T(8,128)} %get-tuple-element.11.sums, f32[3,8,256]{2,1,0:T(8,128)} %pad.4.params, f32[4,8,256]{2,1,0:T(8,128)} %pad_maximum_fusion.2.first, f32[4,8,256]{2,1,0:T(8,128)} %pad_maximum_fusion.3.last), custom_call_target="tpu_custom_call" | custom-call | flops 1000000 | bytes 10000000 | tf_op jit(solution)/shard_map/solve_wells/pallas_call | solution.py:458
  59.3 30.6 %cell_residual.1.given = f32[3,8,256,256]{3,2,1,0:T(8,128)} custom-call(s32[8,256]{1,0:T(8,128)} %add_bitcast_fusion.flat_s.flat, s32[8]{0:T(128)} %bitcast.44, s32[8,256]{1,0:T(8,128)} %add_bitcast_fusion.flat_s.flat, s32[8,256]{1,0:T(8,128)} %bitcast.39, f32[8,256]{1,0:T(8,128)} %get-tuple-element.9.perf_press, f32[8,256]{1,0:T(8,128)} %get-tuple-element.10.perf_weight, ...), custom_call_target="tpu_custom_call" | custom-call | flops 100000000 | bytes 60000000 | tf_op jit(solution)/shard_map/cell_residual/pallas_call | solution.py:483
  89.9 0.6 slice_bitcast_fusion.2
  90.5 1.0 copy-done
  91.5 1.0 copy-done.1
  92.4 7.0 %outer_layers.1 = f32[3,8,256,256]{3,2,1,0:T(8,128)} custom-call(f32[3,8,256,256]{3,2,1,0:T(8,128)} %cell_residual.1.given, f32[8,256,256]{2,1,0:T(8,128)} %press.3, f32[2,8,256,256]{3,2,1,0:T(8,128)} %sats.3, f32[8,256,256]{2,1,0:T(8,128)} %perm.3, f32[4,256,256]{2,1,0:T(8,128)} %copy-done, f32[4,256,256]{2,1,0:T(8,128)} %copy-done.1), custom_call_target="tpu_custom_call", output_to_operand_aliasing={{}: (0, {})} | custom-call | flops 10000000 | bytes 8000000 | tf_op jit(solution)/shard_map/outer_layers/pallas_call | solution.py:508
  (20 shorter events, 0.1 us)
Async XLA Ops:
  3.2 8.4 %copy-start.7 = (s32[1,1,8]{2,1,0:T(1,128)S(1)}, s32[1,1,8]{2,1,0:T(1,128)}, u32[]{:S(2)}) copy-start(s32[1,1,8]{2,1,0:T(1,128)} %param.22) | copy-start | bytes 100
  3.2 9.1 %copy-start.4 = (s32[192,8]{0,1:T(8,128)S(1)}, s32[192,8]{0,1:T(8,128)}, u32[]{:S(2)}) copy-start(s32[192,8]{0,1:T(8,128)} %param.23) | copy-start | bytes 18436
  3.2 9.1 %copy-start.2 = (s32[1,1,8,256]{3,2,1,0:T(8,128)S(1)}, s32[1,1,8,256]{3,2,1,0:T(8,128)}, u32[]{:S(2)}) copy-start(s32[1,1,8,256]{3,2,1,0:T(8,128)} %param.18) | copy-start | bytes 24580
  3.2 9.1 %copy-start.3 = (s32[1,1,8,256]{3,2,1,0:T(8,128)S(1)}, s32[1,1,8,256]{3,2,1,0:T(8,128)}, u32[]{:S(2)}) copy-start(s32[1,1,8,256]{3,2,1,0:T(8,128)} %param.19) | copy-start | bytes 24580
  3.2 9.7 %copy-start.5 = (f32[192,8]{0,1:T(8,128)S(1)}, f32[192,8]{0,1:T(8,128)}, u32[]{:S(2)}) copy-start(f32[192,8]{0,1:T(8,128)} %param.25) | copy-start | bytes 18436
  3.3 9.7 %copy-start.6 = (f32[192,8]{0,1:T(8,128)S(1)}, f32[192,8]{0,1:T(8,128)}, u32[]{:S(2)}) copy-start(f32[192,8]{0,1:T(8,128)} %param.24) | copy-start | bytes 18436
  3.4 87.1 %collective-permute-start = (f32[4,256,256]{2,1,0:T(8,128)S(1)}, f32[4,256,256]{2,1,0:T(8,128)S(1)}, u32[]{:S(2)}, u32[]{:S(2)}) collective-permute-start(f32[4,256,256]{2,1,0:T(8,128)S(1)} %pad_maximum_fusion), channel_id=1, source_target_pairs={{0,1},{1,2},{2,3},{4,5},{5,6},{6,7},{8,9},{9,10},{10,11},{12,13},{... | collective-permute-start | bytes 3145736 | tf_op jit(solution)/shard_map/ppermute | solution.py:424
  8.5 81.9 %collective-permute-start.1 = (f32[4,256,256]{2,1,0:T(8,128)}, f32[4,256,256]{2,1,0:T(8,128)S(1)}, u32[]{:S(2)}, u32[]{:S(2)}) collective-permute-start(f32[4,256,256]{2,1,0:T(8,128)} %pad_maximum_fusion.1), channel_id=1, source_target_pairs={{1,0},{2,1},{3,2},{5,4},{6,5},{7,6},{9,8},{10,9},{11,10},{13,12},{... | collective-permute-start | bytes 3145736 | tf_op jit(solution)/shard_map/ppermute | solution.py:425
  59.3 30.6 %copy-start.8 = (f32[2,256]{1,0:T(2,128)S(1)}, f32[2,256]{1,0:T(2,128)}, u32[]{:S(2)}) copy-start(f32[2,256]{1,0:T(2,128)} %get-tuple-element.15) | copy-start | bytes 6148
  90.5 1.0 copy-start
  91.5 1.0 copy-start.1
where the time goes:
time: 99.4 us; the launch traced here: 99.5 us
  Pallas kernels  81.1 us (82%)
  local copies, waits for them, and re-layouts  9.22 us (9%)
  starting transfers between devices  5.38 us (5%)
  other arithmetic  3.01 us (3%)
    pallas_call x1, Pallas kernels, on_device(): pl.pallas_call(functools.partial(residual_kernel, slab, width, 16, groups...  30.6 us
    pallas_call x1, Pallas kernels, on_device(): pl.pallas_call(functools.partial(gather_kernel, slab, width, halves), out...  24.2 us
    pallas_call x1, Pallas kernels, on_device(): pl.pallas_call(functools.partial(wells_kernel, groups, layers, slab, widt...  19.3 us
    pallas_call x1, Pallas kernels, on_device(): pl.pallas_call(functools.partial(ends_kernel, depth), grid=(2, nx // part...  7.02 us
    ppermute x1, starting transfers between devices, on_device(): below = lax.ppermute(top, 'layer', up)  4.1 us
    unnamed x18, local copies, waits for them, and re-layouts  2.01 us
  transfers between devices with their start and end apart: 2, of which 0 were waited for; matrix products, arithmetic and copies ran while one was open for 8% of the time, Pallas kernels for 74%

commit v1 on v0

v1 whole, which is shorter than its diff:
```python
import functools

import jax
import jax.numpy as jnp
from jax import lax
from jax.experimental import pallas as pl
from jax.experimental.pallas import tpu as pltpu
from jax.sharding import PartitionSpec as P

BLOCK = 128
LANES = 128

MU_WATER = 0.5
MU_OIL = 2.0
MU_GAS = 0.2
GRAVITY = (0.35, 0.28, 0.07)
GEOMETRY = (0.4, 1.0, 1.0)
RELAX = 20.0

VMEM = pltpu.VMEM
SMEM = pltpu.SMEM
MESH = pl.DeviceIdType.MESH
VLIMIT = 56 * 1024 * 1024


def mobilities(water, gas_sat):
    oil_sat = 1.0 - water - gas_sat
    return (
        water * water * (1.0 / MU_WATER),
        oil_sat * oil_sat * (1.0 / MU_OIL),
        gas_sat * gas_sat * (1.0 / MU_GAS),
    )


def pieces(value):
    high = value.astype(jnp.bfloat16).astype(jnp.float32)
    rest = value - high
    mid = rest.astype(jnp.bfloat16).astype(jnp.float32)
    return high, mid, rest - mid


def panel_index(seg, slab, width):
    return (seg % slab) * width + seg // slab


def tall(value, rows):
    return jnp.concatenate(
        [value, jnp.zeros((rows - value.shape[0], value.shape[1]), value.dtype)], axis=0
    )


def split(value, size):
    if size & (size - 1) == 0:
        return lax.shift_right_logical(value, size.bit_length() - 1), value & (size - 1)
    return value // size, value % size


def column_part(row, part, halves):
    value = row[:, :LANES]
    for h in range(1, halves):
        value = jnp.where(part == h, row[:, h * LANES : (h + 1) * LANES], value)
    return value


def gather_kernel(
    slab, width, halves, flat_s, blocks_s, press, sats, flat, seg, index, blocks,
    sums, perf_press, perf_weight, rows,
):
    groups, slots = flat.shape
    for owner in range(groups):
        for block in range(slots // BLOCK):
            base = owner * slots + block * BLOCK

            @pl.when(blocks_s[owner] > block)
            def _(base=base, owner=owner, block=block):
                def step(i, carry):
                    for j in range(16):
                        at = i * 16 + j
                        number, column = split(flat_s[owner, block * BLOCK + at], halves * LANES)
                        row = pl.ds(number, 1)
                        part = split(column, LANES)[0]
                        here = pl.ds(base + at, 1)
                        rows[0, here, :] = column_part(press[row, :], part, halves)
                        rows[1, here, :] = column_part(sats[0, row, :], part, halves)
                        rows[2, here, :] = column_part(sats[1, row, :], part, halves)
                    return carry

                lax.fori_loop(0, BLOCK // 16, step, 0)

    lanes_t = jnp.transpose(tall(flat[...] % LANES, LANES))
    lane = lax.broadcasted_iota(jnp.int32, (slots, LANES), 1)
    picked = jnp.zeros((slots, LANES), jnp.float32)
    for owner in range(groups):
        mask = lane == lanes_t[:, owner : owner + 1]
        for field in range(3):
            row = rows[field, owner * slots : (owner + 1) * slots, :]
            value = jnp.sum(jnp.where(mask, row, 0.0), axis=1, keepdims=True)
            picked = jnp.where(lane == field * groups + owner, value, picked)
    picked = jnp.transpose(picked)
    live = lax.broadcasted_iota(jnp.int32, (groups, slots), 1) < blocks[...] * BLOCK
    pressure = jnp.where(live, picked[0:groups], 0.0)
    water = picked[groups : 2 * groups]
    gas_sat = picked[2 * groups : 3 * groups]
    weight = jnp.where(live, index[...], 0.0)
    lam = mobilities(water, gas_sat)
    mobile = jnp.where(live, weight * lam[0] + weight * lam[1] + weight * lam[2], 0.0)
    perf_press[...] = pressure
    perf_weight[...] = weight
    parts = pieces(mobile) + pieces(mobile * pressure)
    target = panel_index(seg[...], slab, width)
    bins = lax.broadcasted_iota(jnp.int32, (slab * width, slots), 0)
    zero = jnp.zeros((2, slots), jnp.float32)
    chunks = slab * width // LANES
    for owner in range(groups):
        left = jnp.concatenate([part[owner : owner + 1] for part in parts] + [zero], axis=0)
        hot = jnp.where(bins == target[owner : owner + 1], 1.0, 0.0).astype(jnp.bfloat16)
        total = lax.dot_general(
            left.astype(jnp.bfloat16), hot, (((1,), (1,)), ((), ())),
            preferred_element_type=jnp.float32,
        )
        for kind in range(2):
            line = total[3 * kind : 3 * kind + 1] + total[3 * kind + 1 : 3 * kind + 2]
            line = line + total[3 * kind + 2 : 3 * kind + 3]
            for c in range(chunks):
                sums[owner, kind * chunks + c : kind * chunks + c + 1, :] = line[
                    :, c * LANES : (c + 1) * LANES
                ]


def face_terms(geometry, left, right, kinds):
    trans = (geometry * 2.0) * (left[1] * right[1]) / (left[1] + right[1])
    drop = left[0] - right[0]
    if kinds is None:
        up = drop > 0
        flow = trans * drop
        return [flow * jnp.where(up, left[2][a], right[2][a]) for a in range(3)]
    out = []
    for a in range(3):
        potential = drop + kinds[a]
        out.append(trans * potential * jnp.where(potential > 0, left[2][a], right[2][a]))
    return out


def flow_kernel(
    groups, layers, slab, width, chunk, sums, params, press, sats, perm, old, pore,
    out, below, over, table, own_slab, edges,
    got, panel, solved, back, rims, halos, lower,
    send_a, recv_a, send_l, recv_l, send_p, recv_p, send_x, recv_x, send_z, recv_z,
):
    level = pl.program_id(0)
    depth, nx, ny = press.shape
    area = lax.axis_index("areal")
    layer = lax.axis_index("layer")
    nseg = layers * slab
    half = width // LANES

    def areal_peer(d):
        return {"areal": lax.rem(area + d, groups)}

    def layer_peer(d):
        return {"layer": lax.rem(layer + d, layers)}

    def remote(source, target, send, recv, peer):
        return pltpu.make_async_remote_copy(
            source, target, send, recv, device_id=peer, device_id_type=MESH
        )

    def to_owner(d):
        return remote(
            sums.at[lax.rem(area + d, groups)], got.at[d], send_a.at[d], recv_a.at[d], areal_peer(d)
        )

    def to_layer(d):
        return remote(
            panel.at[layer], panel.at[layer], send_l.at[d], recv_l.at[d], layer_peer(d)
        )

    def to_source(d):
        return remote(back.at[area], back.at[area], send_p.at[d], recv_p.at[d], areal_peer(d))

    def rim(side):
        return remote(
            rims.at[side], halos.at[side], send_x.at[side], recv_x.at[side],
            areal_peer(groups - 1 if side else 1),
        )

    def planes(side):
        at = 0 if side else depth - 1
        target = over if side else below
        peer = layer_peer(layers - 1 if side else 1)
        fields = (press.at[at], sats.at[0, at], sats.at[1, at], perm.at[at])
        return [
            remote(fields[f], target.at[f], send_z.at[side, f], recv_z.at[side, f], peer)
            for f in range(4)
        ]

    @pl.when(level == 0)
    def _():
        barrier = pltpu.get_barrier_semaphore()
        for d in range(1, groups):
            pl.semaphore_signal(barrier, inc=1, device_id=areal_peer(d), device_id_type=MESH)
        for d in range(1, layers):
            pl.semaphore_signal(barrier, inc=1, device_id=layer_peer(d), device_id_type=MESH)
        for side in range(2):
            row = slice(0, 1) if side else slice(nx - 1, nx)
            for i in range(depth):
                for f, value in enumerate(
                    (press[i, row, :], sats[0, i, row, :], sats[1, i, row, :], perm[i, row, :])
                ):
                    rims[side, f, i : i + 1, :] = value
        lower[...] = jnp.zeros_like(lower)
        pl.semaphore_wait(barrier, groups + layers - 2)
        for d in range(1, groups):
            to_owner(d).start()
        for side in range(2):
            rim(side).start()

        @pl.when(layer < layers - 1)
        def _():
            for copy in planes(0):
                copy.start()

        @pl.when(layer > 0)
        def _():
            for copy in planes(1):
                copy.start()

    @pl.when(level == 1)
    def _():
        total = sums[area]
        for d in range(1, groups):
            to_owner(d).wait_recv()
            total = total + got[d]
        panel[layer] = total
        for d in range(1, layers):
            to_layer(d).start()

    @pl.when(level == depth - 2)
    def _():
        for d in range(1, layers):
            remote(
                panel.at[layer], panel.at[lax.rem(layer + layers - d, layers)],
                send_l.at[d], recv_l.at[d], layer_peer(d),
            ).wait_recv()

        def lines(kind):
            result = []
            for j in range(layers):
                tile = panel[j]
                for s in range(slab):
                    at = (kind * slab + s) * half
                    result.append(
                        jnp.concatenate([tile[at + h : at + h + 1] for h in range(half)], axis=1)
                    )
            return jnp.concatenate(result, axis=0)

        excess = lines(0) + RELAX
        right = lines(1) + RELAX * params[2]
        parent = params[0]
        cond = params[1]
        place = lax.broadcasted_iota(jnp.int32, (nseg, width), 0).astype(jnp.float32)
        inverse = [None] * nseg
        hits = [None] * nseg
        for s in range(nseg - 1, 0, -1):
            c = cond[s : s + 1]
            e = excess[s : s + 1]
            inverse[s] = 1.0 / (e + c)
            ratio = c * inverse[s]
            hits[s] = place == parent[s : s + 1]
            excess = excess + jnp.where(hits[s], ratio * e, 0.0)
            right = right + jnp.where(hits[s], ratio * right[s : s + 1], 0.0)
        answer = jnp.where(place == 0.0, right[0:1] / excess[0:1], 0.0)
        for s in range(1, nseg):
            above = jnp.sum(jnp.where(hits[s], answer, 0.0), axis=0, keepdims=True)
            value = (right[s : s + 1] + cond[s : s + 1] * above) * inverse[s]
            answer = jnp.where(place == float(s), value, answer)
        for j in range(layers):
            solved[j] = answer[j * slab : (j + 1) * slab]
        back[area] = solved[layer]
        for d in range(1, groups):
            to_source(d).start()

    above = jnp.minimum(level + 1, depth - 1)
    inner = jnp.where(level + 1 < depth, GEOMETRY[0], 0.0)
    carry = [jnp.zeros((1, ny), jnp.float32)] * 3
    column = lax.broadcasted_iota(jnp.int32, (chunk, ny), 1)
    for x in range(0, nx, chunk):
        span = slice(x, x + chunk)
        p = press[level, span, :]
        water = sats[0, level, span, :]
        gas_sat = sats[1, level, span, :]
        k = perm[level, span, :]
        lam = mobilities(water, gas_sat)
        here = (p, k, lam)
        y = min(x + chunk, nx - 1)
        row = slice(y, y + 1)
        next_k = perm[level, row, :] if x + chunk < nx else jnp.zeros((1, ny), jnp.float32)
        next_lam = mobilities(sats[0, level, row, :], sats[1, level, row, :])

        def shifted(value, end):
            return jnp.concatenate([value[1:], end], axis=0)

        there = (
            shifted(p, press[level, row, :]),
            shifted(k, next_k),
            tuple(shifted(lam[a], next_lam[a]) for a in range(3)),
        )
        flux = face_terms(GEOMETRY[1], here, there, None)
        total = []
        for a in range(3):
            total.append(flux[a] - jnp.concatenate([carry[a], flux[a][:-1]], axis=0))
        carry = [flux[a][chunk - 1 :] for a in range(3)]
        there = (
            pltpu.roll(p, ny - 1, 1),
            jnp.where(column < ny - 1, pltpu.roll(k, ny - 1, 1), 0.0),
            tuple(pltpu.roll(lam[a], ny - 1, 1) for a in range(3)),
        )
        flux = face_terms(GEOMETRY[2], here, there, None)
        for a in range(3):
            total[a] = total[a] + (flux[a] - pltpu.roll(flux[a], 1, 1))
        there = (
            press[above, span, :],
            perm[above, span, :],
            mobilities(sats[0, above, span, :], sats[1, above, span, :]),
        )
        flux = face_terms(inner, here, there, GRAVITY)
        volume = pore[0, span, :]
        old_water = old[0, 0, span, :]
        old_gas = old[1, 0, span, :]
        change = (
            water - old_water,
            (1.0 - water - gas_sat) - (1.0 - old_water - old_gas),
            gas_sat - old_gas,
        )
        for a in range(3):
            net = total[a] + (flux[a] - lower[a, span, :])
            lower[a, span, :] = flux[a]
            out[a, 0, span, :] = volume * change[a] + net

    @pl.when(level == depth - 1)
    def _():
        for side in range(2):
            rim(side).wait()

        def side_of(ref, side):
            return (
                ref[side, 0], ref[side, 3], mobilities(ref[side, 1], ref[side, 2])
            )

        low = face_terms(GEOMETRY[1], side_of(halos, 0), side_of(rims, 1), None)
        high = face_terms(GEOMETRY[1], side_of(rims, 0), side_of(halos, 1), None)
        for a in range(3):
            edges[a] = jnp.where(area > 0, low[a], 0.0)
            edges[3 + a] = jnp.where(area < groups - 1, high[a], 0.0)
        for d in range(1, groups):
            remote(
                back.at[area], back.at[lax.rem(area + groups - d, groups)],
                send_p.at[d], recv_p.at[d], areal_peer(d),
            ).wait_recv()
        table[...] = back[...]
        own_slab[...] = solved[layer]
        for d in range(1, groups):
            to_owner(d).wait_send()
            to_source(d).wait_send()
        for d in range(1, layers):
            to_layer(d).wait_send()

        @pl.when(layer < layers - 1)
        def _():
            for copy in planes(0):
                copy.wait_send()
            for copy in planes(1):
                copy.wait_recv()

        @pl.when(layer > 0)
        def _():
            for copy in planes(1):
                copy.wait_send()
            for copy in planes(0):
                copy.wait_recv()


def finish_kernel(
    slab, width, chunk, layers,
    flat_s, blocks_s, flat, seg, perf_press, perf_weight, table, edges, below, over,
    base_in, sats, press, perm, out, source, source_b, adds,
):
    level = pl.program_id(0)
    depth = pl.num_programs(0)
    nx, ny = press.shape[1:]
    groups, slots = flat.shape
    layer = lax.axis_index("layer")

    @pl.when(level == 0)
    def _():
        source[...] = jnp.zeros_like(source)
        source_b[...] = jnp.zeros_like(source_b)
        target = panel_index(seg[...], slab, width)
        bins = lax.broadcasted_iota(jnp.int32, (slab * width, slots), 0)
        found = []
        for owner in range(groups):
            tab = table[owner]
            line = jnp.concatenate([tab[s : s + 1] for s in range(slab)], axis=1)
            left = jnp.concatenate(
                list(pieces(line)) + [jnp.zeros((5, slab * width), jnp.float32)], axis=0
            )
            hot = jnp.where(bins == target[owner : owner + 1], 1.0, 0.0).astype(jnp.bfloat16)
            value = jnp.dot(left.astype(jnp.bfloat16), hot, preferred_element_type=jnp.float32)
            found.append(value[0:1] + value[1:2] + value[2:3])
        rate = perf_weight[...] * (perf_press[...] - jnp.concatenate(found, axis=0))
        rate_t = jnp.transpose(tall(rate, LANES))
        lanes_t = jnp.transpose(tall(flat[...] % ny, LANES))
        lane = lax.broadcasted_iota(jnp.int32, (slots, ny), 1)
        for owner in range(groups):
            adds[owner * slots : (owner + 1) * slots, :] = jnp.where(
                lane == lanes_t[:, owner : owner + 1], rate_t[:, owner : owner + 1], 0.0
            )
        for owner in range(groups):
            for block in range(slots // BLOCK):
                base = owner * slots + block * BLOCK

                @pl.when(blocks_s[owner] > block)
                def _(base=base, owner=owner, block=block):
                    def step(i, carry):
                        for j in range(16):
                            at = i * 16 + j
                            number = split(flat_s[owner, block * BLOCK + at], ny)[0]
                            row = pl.ds(number, 1)
                            into = source if j % 2 == 0 else source_b
                            into[row, :] = into[row, :] + adds[pl.ds(base + at, 1), :]
                        return carry

                    lax.fori_loop(0, BLOCK // 16, step, 0)

    row_from = pl.multiple_of(level * nx, nx)
    for x in range(0, nx, chunk):
        span = slice(x, x + chunk)
        lam = mobilities(sats[0, 0, span, :], sats[1, 0, span, :])
        rows = pl.ds(row_from + x, chunk)
        well = source[rows, :] + source_b[rows, :]
        for a in range(3):
            out[a, 0, span, :] = base_in[a, 0, span, :] + lam[a] * well
    for a in range(3):
        out[a, 0, 0:1, :] = out[a, 0, 0:1, :] - edges[a, pl.ds(level, 1), :]
        out[a, 0, nx - 1 : nx, :] = out[a, 0, nx - 1 : nx, :] + edges[3 + a, pl.ds(level, 1), :]

    def ends(halo, real, sign):
        for x in range(0, nx, chunk):
            span = slice(x, x + chunk)
            here = (press[0, span, :], perm[0, span, :], mobilities(sats[0, 0, span, :], sats[1, 0, span, :]))
            there = (halo[0, span, :], halo[3, span, :], mobilities(halo[1, span, :], halo[2, span, :]))
            pair = (here, there) if sign > 0 else (there, here)
            flux = face_terms(GEOMETRY[0], pair[0], pair[1], GRAVITY)
            for a in range(3):
                out[a, 0, span, :] = out[a, 0, span, :] + sign * jnp.where(real, flux[a], 0.0)

    @pl.when(level == 0)
    def _():
        ends(below, layer > 0, -1.0)

    @pl.when(level == depth - 1)
    def _():
        ends(over, layer < layers - 1, 1.0)


def on_device(
    pressure,
    saturations,
    old_saturations,
    permeability,
    pore_volume,
    perf_cell,
    perf_layer,
    perf_seg,
    perf_index,
    perf_blocks,
    seg_parent,
    seg_cond,
    seg_target,
):
    f32 = jnp.float32
    depth, nx, ny = pressure.shape
    groups, slots = perf_cell.shape[2:]
    layers = lax.axis_size("layer")
    wells, nseg = seg_parent.shape
    slab = nseg // layers
    width = -(-wells // LANES) * LANES
    halves = ny // LANES
    shape = jax.ShapeDtypeStruct
    vm = pl.BlockSpec(memory_space=VMEM)
    sm = pl.BlockSpec(memory_space=SMEM)

    flat = perf_layer[0, 0] * (nx * ny) + perf_cell[0, 0]
    seg = perf_seg[0, 0]
    count = perf_blocks[0, 0]
    tiles = 2 * slab * width // LANES
    sums, perf_press, perf_weight = pl.pallas_call(
        functools.partial(gather_kernel, slab, width, halves),
        out_shape=(
            shape((groups, tiles, LANES), f32),
            shape((groups, slots), f32),
            shape((groups, slots), f32),
        ),
        in_specs=[sm, sm] + [vm] * 6,
        out_specs=(vm, vm, vm),
        scratch_shapes=[VMEM((3, groups * slots, LANES), f32)],
        compiler_params=pltpu.CompilerParams(vmem_limit_bytes=VLIMIT),
        cost_estimate=pl.CostEstimate(flops=10**7, bytes_accessed=3 * 10**7, transcendentals=0),
        name="gather_perforations",
    )(
        flat, count, pressure.reshape(depth * nx, ny), saturations.reshape(2, depth * nx, ny),
        flat, seg, perf_index[0, 0], count[:, None],
    )

    params = jnp.stack([seg_parent.astype(f32), seg_cond, seg_target]).transpose(0, 2, 1)
    params = jnp.pad(params, ((0, 0), (0, 0), (0, width - wells)), constant_values=1.0)
    dma = pltpu.SemaphoreType.DMA
    anywhere = pl.BlockSpec(memory_space=pl.ANY)
    plane = lambda n: pl.BlockSpec((n, 1, nx, ny), lambda i: (0, i, 0, 0))
    arbitrary = ("arbitrary",)
    base, below, over, table, own_slab, edges = pl.pallas_call(
        functools.partial(flow_kernel, groups, layers, slab, width, 16),
        grid=(depth,),
        out_shape=(
            shape((3, depth, nx, ny), f32),
            shape((4, nx, ny), f32),
            shape((4, nx, ny), f32),
            shape((groups, slab, width), f32),
            shape((slab, width), f32),
            shape((6, depth, ny), f32),
        ),
        in_specs=[vm] * 5 + [plane(2), pl.BlockSpec((1, nx, ny), lambda i: (i, 0, 0))],
        out_specs=(plane(3), anywhere, anywhere, vm, vm, vm),
        scratch_shapes=[
            VMEM((groups, tiles, LANES), f32),
            VMEM((layers, tiles, LANES), f32),
            VMEM((layers, slab, width), f32),
            VMEM((groups, slab, width), f32),
            VMEM((2, 4, depth, ny), f32),
            VMEM((2, 4, depth, ny), f32),
            VMEM((3, nx, ny), f32),
            dma((groups,)), dma((groups,)),
            dma((layers,)), dma((layers,)),
            dma((groups,)), dma((groups,)),
            dma((2,)), dma((2,)),
            dma((2, 4)), dma((2, 4)),
        ],
        compiler_params=pltpu.CompilerParams(
            collective_id=0, has_side_effects=True,
            vmem_limit_bytes=VLIMIT, dimension_semantics=arbitrary,
        ),
        cost_estimate=pl.CostEstimate(flops=10**8, bytes_accessed=6 * 10**7, transcendentals=0),
        name="block_flow",
    )(sums, params, pressure, saturations, permeability, old_saturations, pore_volume)

    end_plane = pl.BlockSpec((1, nx, ny), lambda i: (jnp.where(i == depth - 1, i, 0), 0, 0))
    residual = pl.pallas_call(
        functools.partial(finish_kernel, slab, width, 16, layers),
        grid=(depth,),
        out_shape=shape((3, depth, nx, ny), f32),
        in_specs=[sm, sm] + [vm] * 8 + [plane(3), plane(2), end_plane, end_plane],
        out_specs=plane(3),
        scratch_shapes=[
            VMEM((depth * nx, ny), f32),
            VMEM((depth * nx, ny), f32),
            VMEM((groups * slots, ny), f32),
        ],
        compiler_params=pltpu.CompilerParams(
            vmem_limit_bytes=VLIMIT, dimension_semantics=arbitrary
        ),
        cost_estimate=pl.CostEstimate(flops=10**7, bytes_accessed=2 * 10**7, transcendentals=0),
        name="wells_and_ends",
    )(
        flat, count, flat, seg, perf_press, perf_weight, table, edges, below, over,
        base, saturations, pressure, permeability,
    )
    return residual, own_slab[:, :wells].T


def solution(mesh):
    return jax.shard_map(
        on_device,
        mesh=mesh,
        in_specs=(
            P("layer", "areal", None),
            P(None, "layer", "areal", None),
            P(None, "layer", "areal", None),
            P("layer", "areal", None),
            P("layer", "areal", None),
            P("layer", "areal", None, None),
            P("layer", "areal", None, None),
            P("layer", "areal", None, None),
            P("layer", "areal", None, None),
            P("layer", "areal", None),
            P("areal", None),
            P("areal", None),
            P("areal", None),
        ),
        out_specs=(P(None, "layer", "areal", None), P("areal", "layer")),
        check_vma=False,
    )
```

time: 99.4 us -> 76.4 us (0.77)
  Pallas kernels: 81.1 us -> 70.1 us
  local copies, waits for them, and re-layouts: 9.22 us -> 2.51 us
  starting transfers between devices: 5.38 us -> 0 us
    pallas_call x1, Pallas kernels: 24.2 us -> 12.9 us  [on_device(): pl.pallas_call(functools.partial(gather_kernel, slab, width, halves), out...]
    ppermute x2 -> x0, starting transfers between devices: 5.38 us -> none  [the longest x1 4.1 us: on_device(): below = lax.ppermute(top, 'layer', up)]
    slice x4 -> x0, local copies, waits for them, and re-layouts: 4.04 us -> none  [the longest x1 1.27 us: on_device(): pressure[:1]]
    concatenate x4 -> x0, other arithmetic: 2.4 us -> none  [the longest x1 1.09 us: on_device(): jnp.concatenate([pressure[:1], saturations[:, 0], permeability[:1]], axis=0)]
    unnamed x18 -> x2, local copies, waits for them, and re-layouts: 2.01 us -> 0.01 us
    squeeze x2 -> x0, local copies, waits for them, and re-layouts: 1.29 us -> none  [the longest x1 1.29 us: on_device(): saturations[:, 0]]
    pallas_call x3 -> x2, Pallas kernels: 56.9 us -> 57.2 us  [the longest x1 38.4 us: on_device(): pl.pallas_call(functools.partial(flow_kernel, groups, layers, slab, width...]
  transfers between devices with their start and end apart: 2 -> 0, of which waited for: 0 -> 0; matrix products, arithmetic and copies ran while one was open for 8% -> 0% of each run, Pallas kernels for 74% -> 0%
where the time goes in v1:
time: 76.4 us; the launch traced here: 76 us
  Pallas kernels  70.1 us (92%)
  other arithmetic  2.72 us (4%)
  local copies, waits for them, and re-layouts  2.51 us (3%)
    pallas_call x1, Pallas kernels, on_device(): pl.pallas_call(functools.partial(flow_kernel, groups, layers, slab, width...  38.4 us
    pallas_call x1, Pallas kernels, on_device(): pl.pallas_call(functools.partial(finish_kernel, slab, width, 16, layers),...  18.8 us
    pallas_call x1, Pallas kernels, on_device(): pl.pallas_call(functools.partial(gather_kernel, slab, width, halves), out...  12.9 us

profile of v1, /device:TPU:1, one launch (start us, length us, event | category | flops | bytes accessed | tf_op | source)
XLA Modules:
  0.0 76.0 jit_solution(8034287920572023732)
XLA Ops:
  0.6 1.3 %copy.15.blocks = s32[8,1]{1,0:T(8,128)} copy(s32[8,1]{0,1:T(1,128)} %bitcast.23) | data formatting | bytes 64 | tf_op jit(solution)/shard_map/broadcast_in_dim;squeeze | solution.py:512
  1.9 1.3 %add_bitcast_fusion.flat_s.flat = s32[8,256]{1,0:T(8,128)} fusion(s32[1,1,8,256]{3,2,1,0:T(8,128)} %param.18, s32[1,1,8,256]{3,2,1,0:T(8,128)} %param.19), kind=kLoop, calls=%fused_computation.2 | loop fusion | flops 4096 | bytes 24576 | tf_op jit(solution)/shard_map/add | solution.py:493
  3.3 0.7 convert_bitcast_fusion
  4.0 0.7 maximum_bitcast_fusion
  4.7 0.6 pad.4.params
  5.3 12.9 %gather_perforations.1 = (f32[8,8,128]{2,1,0:T(8,128)}, f32[8,256]{1,0:T(8,128)}, f32[8,256]{1,0:T(8,128)}) custom-call(s32[8,256]{1,0:T(8,128)} %add_bitcast_fusion.flat_s.flat, s32[8]{0:T(128)} %bitcast.24, f32[2048,256]{1,0:T(8,128)} %bitcast.17, f32[2,2048,256]{2,1,0:T(8,128)} %bitcast.16, s32[8,256]{1,0:T(8,128)} %add_bitcast_fusion.flat_s.flat, ...), custom_call_target="tpu_custom_call" | custom-call | flops 10000000 | bytes 30000000 | tf_op jit(solution)/shard_map/gather_perforations/pallas_call | solution.py:497
  18.2 38.4 %block_flow.1 = (f32[3,8,256,256]{3,2,1,0:T(8,128)}, f32[4,256,256]{2,1,0:T(8,128)}, f32[4,256,256]{2,1,0:T(8,128)}, f32[8,2,256]{2,1,0:T(2,128)}, f32[2,256]{1,0:T(2,128)}, /*index=5*/f32[6,8,256]{2,1,0:T(8,128)}) custom-call(f32[8,8,128]{2,1,0:T(8,128)} %get-tuple-element.13.sums, f32[3,8,256]{2,1,0:T(8,128)} %pad.4.params, f32[8,256,256]{2,1,0:T(8,128)} %press.3, ...), custom_call_target="tpu_custom_call" | custom-call | flops 100000000 | bytes 60000000 | tf_op jit(solution)/shard_map/block_flow/pallas_call | solution.py:521
  56.6 0.0 copy-start
  56.6 18.8 %wells_and_ends.1 = f32[3,8,256,256]{3,2,1,0:T(8,128)} custom-call(s32[8,256]{1,0:T(8,128)} %add_bitcast_fusion.flat_s.flat, s32[8]{0:T(128)} %bitcast.25, s32[8,256]{1,0:T(8,128)} %add_bitcast_fusion.flat_s.flat, s32[8,256]{1,0:T(8,128)} %bitcast.19, f32[8,256]{1,0:T(8,128)} %get-tuple-element.11.perf_press, f32[8,256]{1,0:T(8,128)} %get-tuple-element.12.perf_weight, ...), custom_call_target="tpu_custom_call" | custom-call | flops 10000000 | bytes 20000000 | tf_op jit(solution)/shard_map/wells_and_ends/pallas_call | solution.py:557
  75.4 0.0 copy-done
  75.4 0.6 slice_bitcast_fusion
Async XLA Ops:
  56.6 18.8 %copy-start = (f32[2,256]{1,0:T(2,128)S(1)}, f32[2,256]{1,0:T(2,128)}, u32[]{:S(2)}) copy-start(f32[2,256]{1,0:T(2,128)} %get-tuple-element.19) | copy-start | bytes 6148

commit v2 on v1

--- a/solution.py
+++ b/solution.py
@@ -63,7 +63,7 @@
 
 
 def gather_kernel(
-    slab, width, halves, flat_s, blocks_s, press, sats, flat, seg, index, blocks,
+    slab, width, halves, flat_s, blocks_s, press, sats, flat, seg, index,
     sums, perf_press, perf_weight, rows,
 ):
     groups, slots = flat.shape
@@ -97,7 +97,11 @@
             value = jnp.sum(jnp.where(mask, row, 0.0), axis=1, keepdims=True)
             picked = jnp.where(lane == field * groups + owner, value, picked)
     picked = jnp.transpose(picked)
-    live = lax.broadcasted_iota(jnp.int32, (groups, slots), 1) < blocks[...] * BLOCK
+    owners = lax.broadcasted_iota(jnp.int32, (groups, slots), 0)
+    limit = jnp.zeros((groups, slots), jnp.int32)
+    for owner in range(groups):
+        limit = jnp.where(owners == owner, blocks_s[owner] * BLOCK, limit)
+    live = lax.broadcasted_iota(jnp.int32, (groups, slots), 1) < limit
     pressure = jnp.where(live, picked[0:groups], 0.0)
     water = picked[groups : 2 * groups]
     gas_sat = picked[2 * groups : 3 * groups]
@@ -142,9 +146,9 @@
 
 
 def flow_kernel(
-    groups, layers, slab, width, chunk, sums, params, press, sats, perm, old, pore,
+    groups, layers, slab, width, chunk, sums, seg_parent, seg_cond, seg_target, press, sats, perm, old, pore,
     out, below, over, table, own_slab, edges,
-    got, panel, solved, back, rims, halos, lower,
+    got, panel, solved, back, rims, halos, lower, wide, wide_parent,
     send_a, recv_a, send_l, recv_l, send_p, recv_p, send_x, recv_x, send_z, recv_z,
 ):
     level = pl.program_id(0)
@@ -184,15 +188,26 @@
             areal_peer(groups - 1 if side else 1),
         )
 
-    def planes(side):
+    def planes(side, fields_of=range(4)):
         at = 0 if side else depth - 1
         target = over if side else below
         peer = layer_peer(layers - 1 if side else 1)
         fields = (press.at[at], sats.at[0, at], sats.at[1, at], perm.at[at])
         return [
             remote(fields[f], target.at[f], send_z.at[side, f], recv_z.at[side, f], peer)
-            for f in range(4)
+            for f in fields_of
         ]
+
+    def start_planes(fields_of):
+        @pl.when(layer < layers - 1)
+        def _():
+            for copy in planes(0, fields_of):
+                copy.start()
+
+        @pl.when(layer > 0)
+        def _():
+            for copy in planes(1, fields_of):
+                copy.start()
 
     @pl.when(level == 0)
     def _():
@@ -214,16 +229,7 @@
             to_owner(d).start()
         for side in range(2):
             rim(side).start()
-
-        @pl.when(layer < layers - 1)
-        def _():
-            for copy in planes(0):
-                copy.start()
-
-        @pl.when(layer > 0)
-        def _():
-            for copy in planes(1):
-                copy.start()
+        start_planes((0, 1))
 
     @pl.when(level == 1)
     def _():
@@ -234,6 +240,7 @@
         panel[layer] = total
         for d in range(1, layers):
             to_layer(d).start()
+        start_planes((2, 3))
 
     @pl.when(level == depth - 2)
     def _():
@@ -255,10 +262,16 @@
             return jnp.concatenate(result, axis=0)
 
         excess = lines(0) + RELAX
-        right = lines(1) + RELAX * params[2]
-        parent = params[0]
-        cond = params[1]
-        place = lax.broadcasted_iota(jnp.int32, (nseg, width), 0).astype(jnp.float32)
+        wells = seg_parent.shape[1]
+        wide[...] = jnp.zeros_like(wide)
+        wide_parent[...] = jnp.zeros_like(wide_parent)
+        wide_parent[:, :wells] = seg_parent[...]
+        wide[0, :, :wells] = seg_cond[...]
+        wide[1, :, :wells] = seg_target[...]
+        right = lines(1) + RELAX * wide[1]
+        parent = wide_parent[...]
+        cond = wide[0]
+        place = lax.broadcasted_iota(jnp.int32, (nseg, width), 0)
         inverse = [None] * nseg
         hits = [None] * nseg
         for s in range(nseg - 1, 0, -1):
@@ -269,11 +282,11 @@
             hits[s] = place == parent[s : s + 1]
             excess = excess + jnp.where(hits[s], ratio * e, 0.0)
             right = right + jnp.where(hits[s], ratio * right[s : s + 1], 0.0)
-        answer = jnp.where(place == 0.0, right[0:1] / excess[0:1], 0.0)
+        answer = jnp.where(place == 0, right[0:1] / excess[0:1], 0.0)
         for s in range(1, nseg):
             above = jnp.sum(jnp.where(hits[s], answer, 0.0), axis=0, keepdims=True)
             value = (right[s : s + 1] + cond[s : s + 1] * above) * inverse[s]
-            answer = jnp.where(place == float(s), value, answer)
+            answer = jnp.where(place == s, value, answer)
         for j in range(layers):
             solved[j] = answer[j * slab : (j + 1) * slab]
         back[area] = solved[layer]
@@ -382,8 +395,9 @@
 
 def finish_kernel(
     slab, width, chunk, layers,
-    flat_s, blocks_s, flat, seg, perf_press, perf_weight, table, edges, below, over,
-    base_in, sats, press, perm, out, source, source_b, adds,
+    flat_s, blocks_s, flat, seg, perf_press, perf_weight, table, own_slab, edges, below, over,
+    base_hbm, sats_hbm, press, perm, out, well_out,
+    source, source_b, adds, base_in, sats, sem,
 ):
     level = pl.program_id(0)
     depth = pl.num_programs(0)
@@ -391,10 +405,20 @@
     groups, slots = flat.shape
     layer = lax.axis_index("layer")
 
+    def fetch(i):
+        return (
+            pltpu.make_async_copy(base_hbm.at[:, i], base_in.at[:, i], sem.at[0, i]),
+            pltpu.make_async_copy(sats_hbm.at[:, i], sats.at[:, i], sem.at[1, i]),
+        )
+
     @pl.when(level == 0)
     def _():
+        for i in range(sem.shape[1]):
+            for copy in fetch(i):
+                copy.start()
         source[...] = jnp.zeros_like(source)
         source_b[...] = jnp.zeros_like(source_b)
+        well_out[...] = own_slab[:, : well_out.shape[1]]
         target = panel_index(seg[...], slab, width)
         bins = lax.broadcasted_iota(jnp.int32, (slab * width, slots), 0)
         found = []
@@ -432,14 +456,16 @@
 
                     lax.fori_loop(0, BLOCK // 16, step, 0)
 
+    for copy in fetch(level):
+        copy.wait()
     row_from = pl.multiple_of(level * nx, nx)
     for x in range(0, nx, chunk):
         span = slice(x, x + chunk)
-        lam = mobilities(sats[0, 0, span, :], sats[1, 0, span, :])
+        lam = mobilities(sats[0, level, span, :], sats[1, level, span, :])
         rows = pl.ds(row_from + x, chunk)
         well = source[rows, :] + source_b[rows, :]
         for a in range(3):
-            out[a, 0, span, :] = base_in[a, 0, span, :] + lam[a] * well
+            out[a, 0, span, :] = base_in[a, level, span, :] + lam[a] * well
     for a in range(3):
         out[a, 0, 0:1, :] = out[a, 0, 0:1, :] - edges[a, pl.ds(level, 1), :]
         out[a, 0, nx - 1 : nx, :] = out[a, 0, nx - 1 : nx, :] + edges[3 + a, pl.ds(level, 1), :]
@@ -447,7 +473,7 @@
     def ends(halo, real, sign):
         for x in range(0, nx, chunk):
             span = slice(x, x + chunk)
-            here = (press[0, span, :], perm[0, span, :], mobilities(sats[0, 0, span, :], sats[1, 0, span, :]))
+            here = (press[0, span, :], perm[0, span, :], mobilities(sats[0, level, span, :], sats[1, level, span, :]))
             there = (halo[0, span, :], halo[3, span, :], mobilities(halo[1, span, :], halo[2, span, :]))
             pair = (here, there) if sign > 0 else (there, here)
             flux = face_terms(GEOMETRY[0], pair[0], pair[1], GRAVITY)
@@ -501,7 +527,7 @@
             shape((groups, slots), f32),
             shape((groups, slots), f32),
         ),
-        in_specs=[sm, sm] + [vm] * 6,
+        in_specs=[sm, sm] + [vm] * 5,
         out_specs=(vm, vm, vm),
         scratch_shapes=[VMEM((3, groups * slots, LANES), f32)],
         compiler_params=pltpu.CompilerParams(vmem_limit_bytes=VLIMIT),
@@ -509,11 +535,9 @@
         name="gather_perforations",
     )(
         flat, count, pressure.reshape(depth * nx, ny), saturations.reshape(2, depth * nx, ny),
-        flat, seg, perf_index[0, 0], count[:, None],
+        flat, seg, perf_index[0, 0],
     )
 
-    params = jnp.stack([seg_parent.astype(f32), seg_cond, seg_target]).transpose(0, 2, 1)
-    params = jnp.pad(params, ((0, 0), (0, 0), (0, width - wells)), constant_values=1.0)
     dma = pltpu.SemaphoreType.DMA
     anywhere = pl.BlockSpec(memory_space=pl.ANY)
     plane = lambda n: pl.BlockSpec((n, 1, nx, ny), lambda i: (0, i, 0, 0))
@@ -529,7 +553,7 @@
             shape((slab, width), f32),
             shape((6, depth, ny), f32),
         ),
-        in_specs=[vm] * 5 + [plane(2), pl.BlockSpec((1, nx, ny), lambda i: (i, 0, 0))],
+        in_specs=[vm] * 7 + [plane(2), pl.BlockSpec((1, nx, ny), lambda i: (i, 0, 0))],
         out_specs=(plane(3), anywhere, anywhere, vm, vm, vm),
         scratch_shapes=[
             VMEM((groups, tiles, LANES), f32),
@@ -539,6 +563,8 @@
             VMEM((2, 4, depth, ny), f32),
             VMEM((2, 4, depth, ny), f32),
             VMEM((3, nx, ny), f32),
+            VMEM((2, nseg, width), f32),
+            VMEM((nseg, width), jnp.int32),
             dma((groups,)), dma((groups,)),
             dma((layers,)), dma((layers,)),
             dma((groups,)), dma((groups,)),
@@ -551,19 +577,22 @@
         ),
         cost_estimate=pl.CostEstimate(flops=10**8, bytes_accessed=6 * 10**7, transcendentals=0),
         name="block_flow",
-    )(sums, params, pressure, saturations, permeability, old_saturations, pore_volume)
+    )(sums, seg_parent.T, seg_cond.T, seg_target.T, pressure, saturations, permeability, old_saturations, pore_volume)
 
     end_plane = pl.BlockSpec((1, nx, ny), lambda i: (jnp.where(i == depth - 1, i, 0), 0, 0))
-    residual = pl.pallas_call(
+    residual, well_pressure = pl.pallas_call(
         functools.partial(finish_kernel, slab, width, 16, layers),
         grid=(depth,),
-        out_shape=shape((3, depth, nx, ny), f32),
-        in_specs=[sm, sm] + [vm] * 8 + [plane(3), plane(2), end_plane, end_plane],
-        out_specs=plane(3),
+        out_shape=(shape((3, depth, nx, ny), f32), shape((slab, wells), f32)),
+        in_specs=[sm, sm] + [vm] * 9 + [anywhere, anywhere, end_plane, end_plane],
+        out_specs=(plane(3), vm),
         scratch_shapes=[
             VMEM((depth * nx, ny), f32),
             VMEM((depth * nx, ny), f32),
             VMEM((groups * slots, ny), f32),
+            VMEM((3, depth, nx, ny), f32),
+            VMEM((2, depth, nx, ny), f32),
+            dma((2, depth)),
         ],
         compiler_params=pltpu.CompilerParams(
             vmem_limit_bytes=VLIMIT, dimension_semantics=arbitrary
@@ -571,10 +600,10 @@
         cost_estimate=pl.CostEstimate(flops=10**7, bytes_accessed=2 * 10**7, transcendentals=0),
         name="wells_and_ends",
     )(
-        flat, count, flat, seg, perf_press, perf_weight, table, edges, below, over,
+        flat, count, flat, seg, perf_press, perf_weight, table, own_slab, edges, below, over,
         base, saturations, pressure, permeability,
     )
-    return residual, own_slab[:, :wells].T
+    return residual, well_pressure.T
 
 
 def solution(mesh):

time: 76.4 us -> 64.4 us (0.84)
  Pallas kernels: 70.1 us -> 61.7 us
  local copies, waits for them, and re-layouts: 2.51 us -> 0 us
  other arithmetic: 2.72 us -> 1.32 us
    pallas_call x1, Pallas kernels: 38.4 us -> 32.8 us  [on_device(): pl.pallas_call(functools.partial(flow_kernel, groups, layers, slab, width...]
    pallas_call x1, Pallas kernels: 18.8 us -> 16 us  [on_device(): pl.pallas_call(functools.partial(finish_kernel, slab, width, 16, layers),...]
    another operation x1 -> x0, local copies, waits for them, and re-layouts: 1.32 us -> none  [on_device(): count[:, None]]
where the time goes in v2:
time: 64.4 us; the launch traced here: 63.7 us
  Pallas kernels  61.7 us (96%)
  other arithmetic  1.32 us (2%)
    pallas_call x1, Pallas kernels, on_device(): pl.pallas_call(functools.partial(flow_kernel, groups, layers, slab, width...  32.8 us
    pallas_call x1, Pallas kernels, on_device(): pl.pallas_call(functools.partial(finish_kernel, slab, width, 16, layers),...  16 us
    pallas_call x1, Pallas kernels, on_device(): pl.pallas_call(functools.partial(gather_kernel, slab, width, halves), out...  12.9 us
    add x1, other arithmetic, on_device(): flat = perf_layer[0, 0] * (nx * ny) + perf_cell[0, 0]  1.32 us

profile of v2, /device:TPU:1, one launch (start us, length us, event | category | flops | bytes accessed | tf_op | source)
XLA Modules:
  0.0 63.7 jit_solution(1681704963821807039)
XLA Ops:
  0.6 1.3 %add_bitcast_fusion.flat_s.flat = s32[8,256]{1,0:T(8,128)} fusion(s32[1,1,8,256]{3,2,1,0:T(8,128)} %param.18, s32[1,1,8,256]{3,2,1,0:T(8,128)} %param.19), kind=kLoop, calls=%fused_computation | loop fusion | flops 4096 | bytes 24576 | tf_op jit(solution)/shard_map/add | solution.py:519
  1.9 12.9 %gather_perforations.1 = (f32[8,8,128]{2,1,0:T(8,128)}, f32[8,256]{1,0:T(8,128)}, f32[8,256]{1,0:T(8,128)}) custom-call(s32[8,256]{1,0:T(8,128)} %add_bitcast_fusion.flat_s.flat, s32[8]{0:T(128)} %bitcast.19, f32[2048,256]{1,0:T(8,128)} %bitcast.12, f32[2,2048,256]{2,1,0:T(8,128)} %bitcast.11, s32[8,256]{1,0:T(8,128)} %add_bitcast_fusion.flat_s.flat, ...), custom_call_target="tpu_custom_call" | custom-call | flops 10000000 | bytes 30000000 | tf_op jit(solution)/shard_map/gather_perforations/pallas_call | solution.py:523
  14.8 32.8 %block_flow.1 = (f32[3,8,256,256]{3,2,1,0:T(8,128)}, f32[4,256,256]{2,1,0:T(8,128)}, f32[4,256,256]{2,1,0:T(8,128)}, f32[8,2,256]{2,1,0:T(2,128)}, f32[2,256]{1,0:T(2,128)}, /*index=5*/f32[6,8,256]{2,1,0:T(8,128)}) custom-call(f32[8,8,128]{2,1,0:T(8,128)} %get-tuple-element.15.sums, s32[8,192]{1,0:T(8,128)} %bitcast.16, f32[8,192]{1,0:T(8,128)} %bitcast.17, ...), custom_call_target="tpu_custom_call" | custom-call | flops 100000000 | bytes 60000000 | tf_op jit(solution)/shard_map/block_flow/pallas_call | solution.py:545
  47.7 16.0 %wells_and_ends.1 = (f32[3,8,256,256]{3,2,1,0:T(8,128)}, f32[2,192]{1,0:T(2,128)}) custom-call(s32[8,256]{1,0:T(8,128)} %add_bitcast_fusion.flat_s.flat, s32[8]{0:T(128)} %bitcast.20, s32[8,256]{1,0:T(8,128)} %add_bitcast_fusion.flat_s.flat, s32[8,256]{1,0:T(8,128)} %bitcast.14, f32[8,256]{1,0:T(8,128)} %get-tuple-element.13.perf_press, ...), custom_call_target="tpu_custom_call" | custom-call | flops 10000000 | bytes 20000000 | tf_op jit(solution)/shard_map/wells_and_ends/pallas_call | solution.py:583
